TPU v7x, 128 devices: a whole 4x4x4 slice. The times are simulated.
128 devices in a mesh: exp: 32 (over x, y, core), tp: 4 (over z).
Axes of the slice: x: 4, y: 4, z: 4, core: 2. Of those that a mesh axis runs over, the one named last changes fastest.
Arguments:
- audio_feats: bfloat16 [16384, 1280], P(('exp', 'tp')), may hold values from -6 to 6
- w_audio: bfloat16 [1280, 2048], P(None, 'tp'), may hold values from -0.15625 to 0.15625
- b_audio: float32 [2048], replicated, may hold values from -3 to 3
- segments: int32 [32, 512], P('exp'), may hold values from 0 to 3, never falling along the last dimension, each value on 1 to 256 neighbouring positions
- w_q: bfloat16 [2048, 4096], P(None, 'tp'), may hold values from -0.125 to 0.125
- w_k: bfloat16 [2048, 512], P(None, 'tp'), may hold values from -0.125 to 0.125
- w_v: bfloat16 [2048, 512], P(None, 'tp'), may hold values from -0.125 to 0.125
- w_o: bfloat16 [4096, 2048], P('tp'), may hold values from -0.09375 to 0.09375
- attn_gain: float32 [2048], replicated, may hold values from 0.1 to 1.9
- q_gain: float32 [128], replicated, may hold values from 0.5 to 2
- k_gain: float32 [128], replicated, may hold values from 0.5 to 2
- moe_gain: float32 [2048], replicated, may hold values from 0.1 to 1.9
- w_router: bfloat16 [2048, 128], replicated
- routes: int32 [16384, 8], P(('exp', 'tp')), may hold values from 0 to 127, all different within a row; in each aligned block of 128 rows (0 to 127, 128 to 255, ...) at most 16 rows name the same one
- w_gate_up: bfloat16 [128, 2048, 1536], P(('exp', 'tp')), may hold values from -0.125 to 0.125
- w_down: bfloat16 [128, 768, 2048], P(('exp', 'tp')), may hold values from -0.625 to 0.625
Outputs:
- mixed: bfloat16 [16384, 2048], P(('exp', 'tp'))
Inputs may be any that keep to these rules, and one draw needn't show every extreme that they name: `routes`: among the tokens of one device (aligned blocks of 128 rows) no expert id is named more than 16 times, a bound that some block reaches; the ids of one token differ. `segments`: ids never fall along a sequence; each id holds 1 to 256 positions, some exactly that many.
All inputs are finite; a program needn't handle non-finite values.
Results may differ from a plain program's by a relative error of at most 0.02.
Values may be sent and summed in bfloat16 or wider, within the bound.
No kernel may reach another device: no remote copies, remote signals or barrier semaphores. Data moves between devices by JAX's collectives and lax.ppermute only.
A program may use at most 128 MiB of HBM per device.

v0:
```python
import math

import jax
import jax.numpy as jnp
from jax import lax
from jax.experimental import pallas as pl
from jax.experimental.pallas import tpu as pltpu
from jax.sharding import PartitionSpec as P

EPSILON = 1e-06
ROPE_BASE = 1000000.0
F32 = jnp.float32
BF16 = jnp.bfloat16
VMEM_BYTES = 32 * 1024 * 1024
EXPERT_VMEM_BYTES = 56 * 1024 * 1024


def whole(count):
    return [pl.BlockSpec(memory_space=pltpu.VMEM)] * count


def far(count):
    return [pl.BlockSpec(memory_space=pltpu.HBM)] * count


def in_far(values):
    return [pltpu.with_memory_space_constraint(value, pltpu.HBM) for value in values]


def shift(value, by):
    size = lax.axis_size("tp")
    return lax.ppermute(value, "tp", [(i, (i + by) % size) for i in range(size)])


def rope_tables(seq_len, head_dim):
    half_dim = head_dim // 2
    inv_freq = ROPE_BASE ** (-(jnp.arange(half_dim, dtype=F32) * 2.0) / head_dim)
    angles = jnp.arange(seq_len, dtype=F32)[:, None] * inv_freq[None, :]
    cos, sin = jnp.cos(angles), jnp.sin(angles)
    return jnp.concatenate([cos, cos], axis=1), jnp.concatenate([-sin, sin], axis=1)


def columns_kernel(order, own, left, right, opposite, far_weight, bias, extra, first, second, near, weight, sems):
    sources = (own, left, right, opposite)
    rows = own.shape[0]
    some = second.shape[0] // rows
    copies = [
        pltpu.make_async_copy(source, near.at[place], sems.at[place])
        for place, source in enumerate(sources)
    ]
    last = pltpu.make_async_copy(far_weight, weight, sems.at[4])
    last.start()
    for copy in copies:
        copy.start()
    first[pl.ds(some * rows, extra.shape[0]), :] = extra[...]
    part = bias[pl.ds(order[0], 1), :]
    last.wait()
    for place, copy in enumerate(copies):
        copy.wait()
        product = jnp.dot(near[place], weight[...], preferred_element_type=F32)
        product = (product + part).astype(BF16)
        at = order[place]
        for number in range(2 * some):
            out = (first, second)[number // some]

            @pl.when(at == number)
            def _():
                out[pl.ds(number % some * rows, rows), :] = product


def run_columns(order, pieces, weight, bias, extra):
    rows, depth = pieces[0].shape
    width = weight.shape[1]
    half = jax.ShapeDtypeStruct((2 * rows, width), BF16)
    longer = jax.ShapeDtypeStruct((2 * rows + extra.shape[0], width), BF16)
    return pl.pallas_call(
        columns_kernel,
        in_specs=[pl.BlockSpec(memory_space=pltpu.SMEM)] + far(5) + whole(2),
        out_specs=whole(2),
        out_shape=(longer, half),
        scratch_shapes=[
            pltpu.VMEM((4, rows, depth), BF16),
            pltpu.VMEM(weight.shape, BF16),
            pltpu.SemaphoreType.DMA((5,)),
        ],
        compiler_params=pltpu.CompilerParams(vmem_limit_bytes=VMEM_BYTES),
        cost_estimate=pl.CostEstimate(
            flops=8 * rows * weight.size, transcendentals=0,
            bytes_accessed=2 * weight.size + 8 * pieces[0].size,
        ),
        name="columns",
    )(order, *in_far(pieces[:1]), *pieces[1:], *in_far([weight]), bias, extra)


def chosen_kernel(order, own, left, right, opposite, *outs):
    experts, pairs, rows, columns = outs[0].shape
    cap = rows // 2
    tokens = columns // (2 * pairs)
    some = own.shape[0]
    row = lax.broadcasted_iota(jnp.int32, (some, rows, tokens), 1)
    for place, piece in enumerate((own, left, right, opposite)):
        at = order[place]
        pair = at // 2
        here_columns = pl.ds(pl.multiple_of(at * tokens, tokens), tokens)
        slots = [
            jnp.where(row // cap == at % 2, row % cap + which * cap, -2).astype(F32)
            for which in range(len(outs))
        ]

        def body(part, carry):
            places = piece[:, pl.ds(pl.multiple_of(part * tokens, tokens), tokens)].astype(F32)
            places = jnp.broadcast_to(places[:, None, :], row.shape)
            here = pl.ds(part * some, some)
            for slot, out in zip(slots, outs):
                met = (places == slot).astype(F32).astype(BF16)
                out[here, pair, :, here_columns] = met
                out[here, pairs - 1 - pair, :, here_columns] = jnp.zeros_like(met)
            return carry

        lax.fori_loop(0, experts // some, body, 0)


def run_chosen(order, parts, tokens, experts, cap, count):
    rows, width = parts[0].shape
    some = experts * tokens // width
    table = pl.BlockSpec((some, width), lambda i: (rows // some - 1, 0))
    shape = (experts, 2, 2 * cap // count, 4 * tokens)
    result = pl.BlockSpec(shape, lambda i: (0, 0, 0, 0))
    return pl.pallas_call(
        chosen_kernel,
        grid=(1,),
        in_specs=[pl.BlockSpec(memory_space=pltpu.SMEM)] + [table] * 4,
        out_specs=[result] * count,
        out_shape=(jax.ShapeDtypeStruct(shape, BF16),) * count,
        compiler_params=pltpu.CompilerParams(vmem_limit_bytes=VMEM_BYTES),
        name="chosen",
    )(order, *parts)


def layer_kernel(*refs, first):
    order, sources, refs = refs[0], refs[1:5], refs[5:]
    if first:
        past_keys, past_values = refs[:2]
        refs = refs[2:]
    weights, refs = refs[:4], refs[4:]
    (gain, q_gain, k_gain, cos, sin, seg_col, seg_row,
     to_right, to_left, to_opposite, to_own, keys_out, values_out,
     normed, queries, keys, values, context, near, w_k, w_v, w_q, w_o, sems) = refs
    count, width = to_own.shape
    feat_dim = w_q.shape[0]
    head_dim = w_k.shape[1]
    heads = queries.shape[0]
    block = 128
    factor = float(head_dim) ** -0.5 * math.log2(math.e)

    copies = [
        pltpu.make_async_copy(source.at[pl.ds(0, count), :], near.at[place], sems.at[place])
        for place, source in enumerate(sources)
    ] + [
        pltpu.make_async_copy(source, target, sems.at[4 + place])
        for place, (source, target) in enumerate(zip(weights, (w_k, w_v, w_q, w_o)))
    ]
    for copy in copies:
        copy.start()
    for copy in copies[:4]:
        copy.wait()

    pieces = [near[place].astype(F32) for place in range(4)]
    squares = sum(jnp.sum(piece * piece, axis=1, keepdims=True) for piece in pieces)
    scale = lax.rsqrt(squares / feat_dim + EPSILON)
    for place, piece in enumerate(pieces):
        at = order[place]
        columns = pl.ds(pl.multiple_of(at * width, width), width)
        normed[:, columns] = (piece * scale * gain[:, columns]).astype(BF16)

    here = pl.ds(first, count)
    turn_cos, turn_sin = cos[here, :], sin[here, :]

    def head_of(raw, head_gain):
        squares = jnp.mean(raw * raw, axis=1, keepdims=True)
        raw = raw * lax.rsqrt(squares + EPSILON) * head_gain[...]
        return (raw * turn_cos + pltpu.roll(raw, head_dim // 2, 1) * turn_sin).astype(BF16)

    if first:
        keys[:first, :] = past_keys[...]
        values[:first, :] = past_values[...]
    copies[4].wait()
    new_keys = head_of(jnp.dot(normed[...], w_k[...], preferred_element_type=F32), k_gain)
    copies[5].wait()
    new_values = jnp.dot(normed[...], w_v[...], preferred_element_type=F32).astype(BF16)
    keys[here, :] = new_keys
    values[here, :] = new_values
    keys_out[...] = new_keys
    values_out[...] = new_values
    copies[6].wait()
    for pair in range(heads // 2):
        raw = jnp.dot(
            normed[...], w_q[:, pl.ds(pair * 2 * head_dim, 2 * head_dim)],
            preferred_element_type=F32,
        )
        for one in range(2):
            queries[2 * pair + one] = head_of(raw[:, one * head_dim : (one + 1) * head_dim], q_gain)

    for start in range(0, count, block):
        span = first + start + block
        row_at = first + start + lax.broadcasted_iota(jnp.int32, (block, span), 0)
        col_at = lax.broadcasted_iota(jnp.int32, (block, span), 1)
        same = seg_col[pl.ds(first + start, block), :] == seg_row[:, :span]
        allowed = same & (col_at <= row_at)
        for head in range(heads):
            scores = lax.dot_general(
                queries[head, pl.ds(start, block), :], keys[:span, :], (((1,), (1,)), ((), ())),
                preferred_element_type=F32,
            )
            scores = jnp.where(allowed, scores, -1e30)
            expo = jnp.exp2((scores - jnp.max(scores, axis=1, keepdims=True)) * factor)
            total = jnp.sum(expo, axis=1, keepdims=True)
            mixed = jnp.dot(expo.astype(BF16), values[:span, :], preferred_element_type=F32)
            context[pl.ds(start, block), pl.ds(head * head_dim, head_dim)] = (
                mixed / total
            ).astype(BF16)

    copies[7].wait()
    for place, out in ((2, to_right), (1, to_left), (3, to_opposite), (0, to_own)):
        columns = pl.ds(pl.multiple_of(order[place] * width, width), width)
        out[...] = jnp.dot(context[...], w_o[:, columns], preferred_element_type=F32).astype(BF16)


def run_layer(
    order, parts, count, past, first, gain, w_q, w_k, w_v, w_o, q_gain, k_gain, cos, sin, seg
):
    width = parts[0].shape[1]
    feat_dim = w_q.shape[0]
    head_dim = w_k.shape[1]
    heads = w_q.shape[1] // head_dim
    span = first + count
    piece = jax.ShapeDtypeStruct((count, width), BF16)
    kv = jax.ShapeDtypeStruct((count, head_dim), BF16)
    weights = (w_k, w_v, w_q, w_o)
    operands = [*parts, *past, *in_far(weights), gain, q_gain, k_gain, cos, sin, *seg]

    def kernel(*refs):
        layer_kernel(*refs, first=first)

    return pl.pallas_call(
        kernel,
        in_specs=[pl.BlockSpec(memory_space=pltpu.SMEM)]
        + far(len(parts)) + whole(len(past)) + far(len(weights))
        + whole(len(operands) - len(parts) - len(past) - len(weights)),
        out_specs=whole(6),
        out_shape=(piece,) * 4 + (kv,) * 2,
        scratch_shapes=[
            pltpu.VMEM((count, feat_dim), BF16),
            pltpu.VMEM((heads, count, head_dim), BF16),
            pltpu.VMEM((span, head_dim), BF16),
            pltpu.VMEM((span, head_dim), BF16),
            pltpu.VMEM((count, heads * head_dim), BF16),
            pltpu.VMEM((len(parts), count, width), BF16),
        ]
        + [pltpu.VMEM(weight.shape, BF16) for weight in weights]
        + [pltpu.SemaphoreType.DMA((len(parts) + len(weights),))],
        compiler_params=pltpu.CompilerParams(vmem_limit_bytes=VMEM_BYTES),
        cost_estimate=pl.CostEstimate(
            flops=4 * count * feat_dim * (heads + 1) * head_dim
            + 4 * count * span * heads * head_dim,
            transcendentals=count * span * heads,
            bytes_accessed=4 * feat_dim * (heads + 1) * head_dim + 16 * count * width,
        ),
        name="layer",
    )(order, *operands)


def expert_kernel(rows, gain, w_gate_up, w_down, out, normed):
    groups, parts, slots, width = rows.shape
    count = groups * slots
    feat_dim = parts * width
    inner = w_down.shape[0]
    pieces = [rows[:, part].reshape(count, width).astype(F32) for part in range(parts)]
    squares = sum(jnp.sum(piece * piece, axis=1, keepdims=True) for piece in pieces)
    scale = lax.rsqrt(squares / feat_dim + EPSILON)
    for part, piece in enumerate(pieces):
        normed[:, pl.ds(part * width, width)] = (
            piece * scale * gain[pl.ds(part, 1), :]
        ).astype(BF16)
    both = jnp.dot(normed[...], w_gate_up[...], preferred_element_type=F32)
    gate, up = both[:, :inner], both[:, inner:]
    hidden = (gate * jax.nn.sigmoid(gate) * up).astype(BF16)
    result = jnp.dot(hidden, w_down[...], preferred_element_type=F32)
    out[...] = result.astype(BF16)


def run_experts(arrived, gain, w_gate_up, w_down):
    sources, parts, slots, width = arrived.shape
    feat_dim, double = w_gate_up.shape
    groups = 8

    def fixed(shape):
        return pl.BlockSpec(shape, lambda i: (0, 0), pipeline_mode=pl.Buffered(1))

    return pl.pallas_call(
        expert_kernel,
        grid=(sources // groups,),
        in_specs=[
            pl.BlockSpec((groups, parts, slots, width), lambda i: (i, 0, 0, 0)),
            fixed(gain.shape), fixed(w_gate_up.shape), fixed(w_down.shape),
        ],
        out_specs=pl.BlockSpec((groups * slots, feat_dim), lambda i: (i, 0)),
        out_shape=pltpu.HBM((sources * slots, feat_dim), BF16),
        scratch_shapes=[pltpu.VMEM((groups * slots, feat_dim), BF16)],
        compiler_params=pltpu.CompilerParams(vmem_limit_bytes=EXPERT_VMEM_BYTES),
        cost_estimate=pl.CostEstimate(
            flops=3 * sources * slots * feat_dim * double,
            transcendentals=sources * slots * double // 2,
            bytes_accessed=4 * sources * slots * feat_dim + 3 * feat_dim * double,
        ),
        name="experts",
    )(*in_far([arrived]), gain, *in_far([w_gate_up, w_down]))


def join_kernel(order, own, left, right, opposite, out):
    width = own.shape[1]
    for place, piece in enumerate((own, left, right, opposite)):
        out[:, pl.ds(pl.multiple_of(order[place] * width, width), width)] = piece[...]


def run_join(order, pieces):
    count, width = pieces[0].shape
    return pl.pallas_call(
        join_kernel,
        in_specs=[pl.BlockSpec(memory_space=pltpu.SMEM)] + whole(4),
        out_specs=whole(1)[0],
        out_shape=jax.ShapeDtypeStruct((count, 4 * width), BF16),
        name="join",
    )(order, *pieces)


def on_device(
    audio_feats, w_audio, b_audio, segments, w_q, w_k, w_v, w_o, attn_gain, q_gain, k_gain,
    moe_gain, w_router, routes, w_gate_up, w_down,
):
    me = lax.axis_index("tp")
    tp_size = lax.axis_size("tp")
    tok_rows = audio_feats.shape[0]
    feat_dim = b_audio.shape[0]
    seq_len = segments.shape[1]
    head_dim = q_gain.shape[0]
    experts = w_router.shape[1]
    top_count = routes.shape[1]
    width = w_audio.shape[1]
    slot_cap = max(4, 2 * tok_rows * top_count // experts)
    order = lax.rem(me + jnp.array([0, 3, 1, 2], jnp.int32), tp_size)

    def exchange(value):
        return [value, shift(value, 1), shift(value, -1), shift(value, 2)]

    def in_order(value):
        stack = jnp.zeros((tp_size,) + value.shape, value.dtype)
        for place, piece in enumerate(exchange(value)):
            stack = lax.dynamic_update_slice_in_dim(stack, piece[None], order[place], 0)
        return stack

    expert_ids = jnp.arange(experts, dtype=jnp.int32)
    named = jnp.any(routes[:, :, None] == expert_ids[None, None, :], axis=1)
    token_ids = jnp.arange(tok_rows, dtype=jnp.int32)
    earlier = (token_ids[None, :] < token_ids[:, None]).astype(BF16)
    my_places = jnp.dot(earlier, named.astype(BF16), preferred_element_type=F32)
    my_places = jnp.where(named, my_places, -1.0).astype(BF16)
    groups = width // tok_rows
    extra = my_places.T.reshape(groups, -1, tok_rows).transpose(1, 0, 2).reshape(-1, width)

    chunk_a, chunk_b = run_columns(
        order, exchange(audio_feats), w_audio, b_audio.reshape(tp_size, width), extra
    )
    parts_a = exchange(chunk_a)
    chunk_b, _ = lax.optimization_barrier((chunk_b, parts_a[1]))
    parts_b = exchange(chunk_b)

    cos, sin = rope_tables(seq_len, head_dim)
    seg = (segments.reshape(seq_len, 1), segments)
    by_device = (tp_size, width)
    half = seq_len // 2

    def layer(first, parts, past):
        *pieces, keys, values = run_layer(
            order, parts, half, past, first, attn_gain[None], w_q, w_k, w_v, w_o,
            q_gain[None], k_gain[None], cos, sin, seg,
        )
        return pieces, (keys, values)

    def summands(pieces):
        to_right, to_left, to_opposite, mine = pieces
        return [shift(to_right, 1), shift(to_left, -1), shift(to_opposite, 2), mine]

    pieces_a, past = layer(0, parts_a, ())
    pieces_b, _ = layer(half, parts_b, past)
    tables, pieces_b = lax.optimization_barrier((parts_a, pieces_b))
    count = 2
    met = run_chosen(order, tables, tok_rows, experts, slot_cap, count)
    terms = (summands(pieces_a), summands(pieces_b))
    blocks = jnp.concatenate(
        [
            (sum(piece.astype(F32) for piece in term) + chunk.astype(F32)).astype(BF16)
            for chunk, term in zip((chunk_a[:half], chunk_b), terms)
        ],
        axis=0,
    )

    def travel(rows):
        return lax.all_to_all(rows, ("exp", "tp"), 0, 0, tiled=True)

    results = []
    for chosen in met:
        rows = jnp.dot(chosen.reshape(-1, seq_len), blocks, preferred_element_type=F32)
        arrived = travel(rows.astype(BF16).reshape(experts, -1, width))
        results.append(
            run_experts(
                arrived.reshape(-1, tp_size, arrived.shape[1], width),
                moe_gain.reshape(by_device), w_gate_up[0], w_down[0],
            ).reshape(experts, -1, feat_dim)
        )

    blocks, _ = lax.optimization_barrier((blocks, results[0]))
    blocks = blocks.reshape(tp_size, tok_rows, width)

    def block_of(place):
        return lax.dynamic_index_in_dim(blocks, order[place], 0, keepdims=False)

    own = [block_of(0), shift(block_of(2), 1), shift(block_of(1), -1), shift(block_of(3), 2)]
    results[1], own = lax.optimization_barrier((results[1], own))
    hidden_res = run_join(order, own)
    hidden_res = hidden_res.astype(F32)
    returned = [travel(rows).reshape(-1, feat_dim) for rows in results]
    squares = jnp.mean(hidden_res * hidden_res, axis=-1, keepdims=True)
    normed = (hidden_res * lax.rsqrt(squares + EPSILON) * moe_gain).astype(BF16)

    logits = jnp.dot(normed, w_router, preferred_element_type=F32)
    peak = jnp.max(jnp.where(named, logits, -jnp.inf), axis=1, keepdims=True)
    expo = jnp.where(named, jnp.exp(jnp.minimum(logits - peak, 0.0)), 0.0)
    gates = (expo / jnp.sum(expo, axis=1, keepdims=True)).astype(BF16)
    part_cap = slot_cap // count
    slot_of = jnp.arange(experts * part_cap, dtype=jnp.int32)
    spread = (expert_ids[:, None] == (slot_of // part_cap)[None, :]).astype(BF16)
    wide_gates = jnp.dot(gates, spread, preferred_element_type=F32)
    wide_places = jnp.dot(my_places, spread, preferred_element_type=F32)
    total = hidden_res
    for part in range(count):
        slot = (slot_of % part_cap + part * part_cap).astype(F32)
        combine = jnp.where(wide_places == slot[None, :], wide_gates, 0.0).astype(BF16)
        total = total + jnp.dot(combine, returned[part], preferred_element_type=F32)
    return total.astype(BF16)


def solution(mesh):
    in_specs = (
        P(("exp", "tp"), None),
        P(None, "tp"),
        P(),
        P("exp", None),
        P(None, "tp"),
        P(None, "tp"),
        P(None, "tp"),
        P("tp", None),
        P(),
        P(),
        P(),
        P(),
        P(),
        P(("exp", "tp"), None),
        P(("exp", "tp"), None, None),
        P(("exp", "tp"), None, None),
    )
    out_specs = P(("exp", "tp"), None)
    return jax.shard_map(
        on_device, mesh=mesh, in_specs=in_specs, out_specs=out_specs, check_vma=False
    )
```

profile of v0, /device:TPU:0, one launch (start us, length us, event | category | flops | bytes accessed | tf_op | source)
XLA Modules:
  0.0 329.6 jit_solution(16100436020509553801)
XLA Ops:
  0.0 2.1 collective-permute-start
  2.1 2.2 collective-permute-start.1
  9.2 2.9 collective-permute-done.left
  12.1 6.5 %collective-permute-done.1.right = bf16[128,1280]{1,0:T(8,128)(2,1)S(1)} collective-permute-done((bf16[128,1280]{1,0:T(8,128)(2,1)}, bf16[128,1280]{1,0:T(8,128)(2,1)S(1)}, u32[]{:S(2)}, u32[]{:S(2)}) %collective-permute-start.1) | collective-permute-done | bytes 327712 | tf_op jit(solution)/shard_map/ppermute | solution.py:32
  20.3 3.4 %columns.1 = (bf16[288,512]{1,0:T(8,128)(2,1)S(1)}, bf16[256,512]{1,0:T(8,128)(2,1)S(1)}) custom-call(s32[4]{0:T(128)S(1)} %compare_select_fusion.order.refs_0_, bf16[128,1280]{1,0:T(8,128)(2,1)} %own.1, bf16[128,1280]{1,0:T(8,128)(2,1)S(1)} %collective-permute-done.left, bf16[128,1280]{1,0:T(8,128)(2,1)S(1)} %collective-permute-done.1.right, ...), custom_call_target="tpu_custom_call" | custom-call | flops 671088640 | bytes 2621440 | tf_op jit(solution)/shard_map/columns/pallas_call | solution.py:76
  24.9 2.1 collective-permute-start.4
  28.2 10.5 %collective-permute-done.3.refs_2_.left = bf16[288,512]{1,0:T(8,128)(2,1)S(1)} collective-permute-done((bf16[288,512]{1,0:T(8,128)(2,1)S(1)}, bf16[288,512]{1,0:T(8,128)(2,1)S(1)}, u32[]{:S(2)}, u32[]{:S(2)}) %collective-permute-start.3) | collective-permute-done | bytes 294944 | tf_op jit(solution)/shard_map/ppermute | solution.py:32
  38.7 3.2 collective-permute-start.7
  43.6 8.6 %layer.2 = (bf16[256,512]{1,0:T(8,128)(2,1)S(1)}, bf16[256,512]{1,0:T(8,128)(2,1)S(1)}, bf16[256,512]{1,0:T(8,128)(2,1)S(1)}, bf16[256,512]{1,0:T(8,128)(2,1)S(1...) custom-call(s32[4]{0:T(128)S(1)} %compare_select_fusion.order.refs_0_, ...), custom_call_target="tpu_custom_call" | custom-call | flops 2684354560 | bytes 11534336 | tf_op jit(solution)/shard_map/layer/pallas_call | solution.py:245
  53.9 2.0 collective-permute-start.11
  57.2 10.7 %layer.3 = (bf16[256,512]{1,0:T(8,128)(2,1)S(1)}, bf16[256,512]{1,0:T(8,128)(2,1)S(1)}, bf16[256,512]{1,0:T(8,128)(2,1)S(1)}, bf16[256,512]{1,0:T(8,128)(2,1)S(1...) custom-call(s32[4]{0:T(128)S(1)} %compare_select_fusion.order.refs_0_, ...), custom_call_target="tpu_custom_call" | custom-call | flops 2952790016 | bytes 11534336 | tf_op jit(solution)/shard_map/layer/pallas_call | solution.py:245
  68.2 3.1 collective-permute-start.13
  71.3 2.1 chosen.1
  73.8 1.8 collective-permute-done.12
  75.6 5.7 %collective-permute-done.14 = bf16[256,512]{1,0:T(8,128)(2,1)S(1)} collective-permute-done((bf16[256,512]{1,0:T(8,128)(2,1)S(1)}, bf16[256,512]{1,0:T(8,128)(2,1)S(1)}, u32[]{:S(2)}, u32[]{:S(2)}) %collective-permute-start.14) | collective-permute-done | bytes 262176 | tf_op jit(solution)/shard_map/ppermute | solution.py:32
  81.5 4.4 %convolution_convert_fusion = bf16[4096,512]{1,0:T(8,128)(2,1)} fusion(bf16[4096,512]{1,0:T(8,128)(2,1)S(1)} %bitcast.61, bf16[256,512]{1,0:T(8,128)(2,1)S(1)} %add_convert_fusion, bf16[256,512]{1,0:T(8,128)(2,1)S(1)} %add_convert_fusion.1), kind=kOutput, calls=%fused_computation | convolution fusion | flops 2150629376 | bytes 8912896 | tf_op jit(solution)/shard_map/dot_general | solution.py:413
  85.9 8.5 %all-to-all-start.1 = ((bf16[128,32,512]{2,1,0:T(8,128)(2,1)}), bf16[128,32,512]{2,1,0:T(8,128)(2,1)}, u32[]{:S(2)}, u32[]{:S(2)}) async-start(bf16[128,32,512]{2,1,0:T(8,128)(2,1)} %bitcast.65), calls=%async_computation.1 | async-start | bytes 8388608 | tf_op jit(solution)/shard_map/all_to_all | solution.py:409
  94.3 6.5 %convolution_convert_fusion.1 = bf16[4096,512]{1,0:T(8,128)(2,1)} fusion(bf16[4096,512]{1,0:T(8,128)(2,1)} %bitcast.60, bf16[256,512]{1,0:T(8,128)(2,1)S(1)} %add_convert_fusion, bf16[256,512]{1,0:T(8,128)(2,1)S(1)} %add_convert_fusion.1), kind=kOutput, calls=%fused_computation.1 | convolution fusion | flops 2150629376 | bytes 8912896 | tf_op jit(solution)/shard_map/dot_general | solution.py:413
  100.8 45.6 %all-to-all-done.1 = bf16[128,32,512]{2,1,0:T(8,128)(2,1)} async-done(((bf16[128,32,512]{2,1,0:T(8,128)(2,1)}), bf16[128,32,512]{2,1,0:T(8,128)(2,1)}, u32[]{:S(2)}, u32[]{:S(2)}) %all-to-all-start.1) | async-done | bytes 4194336 | tf_op jit(solution)/shard_map/all_to_all | solution.py:409
  146.4 6.0 %all-to-all-start = ((bf16[128,32,512]{2,1,0:T(8,128)(2,1)}), bf16[128,32,512]{2,1,0:T(8,128)(2,1)}, u32[]{:S(2)}, u32[]{:S(2)}) async-start(bf16[128,32,512]{2,1,0:T(8,128)(2,1)} %bitcast.64), calls=%async_computation | async-start | bytes 8388608 | tf_op jit(solution)/shard_map/all_to_all | solution.py:409
  153.0 16.5 %experts.3 = bf16[1024,2048]{1,0:T(8,128)(2,1)} custom-call(bf16[32,4,32,512]{3,2,1,0:T(8,128)(2,1)} %bitcast.15.rows, f32[4,512]{1,0:T(4,128)} %reshape.102.gain, bf16[2048,1536]{1,0:T(8,128)(2,1)} %bitcast.69, bf16[768,2048]{1,0:T(8,128)(2,1)} %bitcast.71), custom_call_target="tpu_custom_call" | custom-call | flops 9663676416 | bytes 17825792 | tf_op jit(solution)/shard_map/experts/pallas_call | solution.py:300
  169.5 35.1 %all-to-all-done = bf16[128,32,512]{2,1,0:T(8,128)(2,1)} async-done(((bf16[128,32,512]{2,1,0:T(8,128)(2,1)}), bf16[128,32,512]{2,1,0:T(8,128)(2,1)}, u32[]{:S(2)}, u32[]{:S(2)}) %all-to-all-start) | async-done | bytes 4194336 | tf_op jit(solution)/shard_map/all_to_all | solution.py:409
  204.6 5.8 %all-to-all-start.2 = ((bf16[128,8,2048]{2,1,0:T(8,128)(2,1)}), bf16[128,8,2048]{2,1,0:T(8,128)(2,1)}, u32[]{:S(2)}, u32[]{:S(2)}) async-start(bf16[128,8,2048]{2,1,0:T(8,128)(2,1)} %bitcast.62), calls=%async_computation.2 | async-start | bytes 8388608 | tf_op jit(solution)/shard_map/all_to_all | solution.py:409
  220.3 2.2 collective-permute-start.16
  224.1 16.4 %experts.2 = bf16[1024,2048]{1,0:T(8,128)(2,1)} custom-call(bf16[32,4,32,512]{3,2,1,0:T(8,128)(2,1)} %bitcast.9.rows, f32[4,512]{1,0:T(4,128)} %reshape.102.gain, bf16[2048,1536]{1,0:T(8,128)(2,1)} %bitcast.70, bf16[768,2048]{1,0:T(8,128)(2,1)} %bitcast.72), custom_call_target="tpu_custom_call" | custom-call | flops 9663676416 | bytes 17825792 | tf_op jit(solution)/shard_map/experts/pallas_call | solution.py:300
  240.5 19.8 %collective-permute-done.15.left = bf16[128,512]{1,0:T(8,128)(2,1)S(1)} collective-permute-done((bf16[128,512]{1,0:T(8,128)(2,1)S(1)}, bf16[128,512]{1,0:T(8,128)(2,1)S(1)}, u32[]{:S(2)}, u32[]{:S(2)}) %collective-permute-start.15) | collective-permute-done | bytes 131104 | tf_op jit(solution)/shard_map/ppermute | solution.py:32
  260.3 3.7 %collective-permute-done.17.opposite = bf16[128,512]{1,0:T(8,128)(2,1)S(1)} collective-permute-done((bf16[128,512]{1,0:T(8,128)(2,1)S(1)}, bf16[128,512]{1,0:T(8,128)(2,1)S(1)}, u32[]{:S(2)}, u32[]{:S(2)}) %collective-permute-start.17) | collective-permute-done | bytes 131104 | tf_op jit(solution)/shard_map/ppermute | solution.py:32
  264.7 8.9 %all-to-all-start.3 = ((bf16[128,8,2048]{2,1,0:T(8,128)(2,1)}), bf16[128,8,2048]{2,1,0:T(8,128)(2,1)}, u32[]{:S(2)}, u32[]{:S(2)}) async-start(bf16[128,8,2048]{2,1,0:T(8,128)(2,1)} %bitcast.63), calls=%async_computation.3 | async-start | bytes 8388608 | tf_op jit(solution)/shard_map/all_to_all | solution.py:409
  273.9 1.9 join.1
  278.9 3.0 fusion.4
  281.9 43.9 %all-to-all-done.3 = bf16[128,8,2048]{2,1,0:T(8,128)(2,1)} async-done(((bf16[128,8,2048]{2,1,0:T(8,128)(2,1)}), bf16[128,8,2048]{2,1,0:T(8,128)(2,1)}, u32[]{:S(2)}, u32[]{:S(2)}) %all-to-all-start.3) | async-done | bytes 4194336 | tf_op jit(solution)/shard_map/all_to_all | solution.py:409
  325.9 3.7 %fusion.10 = bf16[128,2048]{1,0:T(8,128)(2,1)} fusion(f32[128,2048]{1,0:T(8,128)S(1)} %fusion.4, bf16[128,8,2048]{2,1,0:T(8,128)(2,1)} %all-to-all-done.3, bf16[128,1024]{1,0:T(8,128)(2,1)S(1)} %fusion.21, f32[128,1024]{1,0:T(8,128)S(1)} %fusion.22, f32[1024]{0:T(1024)S(1)} %fusion.45), kind=kOutput, calls=%fused_computation.8 | convolution fusion | flops 537657344 | bytes 6557696 | tf_op jit(solution)/shard_map/dot_general | solution.py:449
  (80 shorter events, 23.0 us)
Async XLA Ops:
  0.0 277.1 %copy-start = (bf16[2048,128]{1,0:T(8,128)(2,1)S(1)}, bf16[2048,128]{1,0:T(8,128)(2,1)}, u32[]{:S(2)}) copy-start(bf16[2048,128]{1,0:T(8,128)(2,1)} %param.29) | copy-start | bytes 1572868
  0.0 42.1 %copy-start.3 = (s32[1,512]{1,0:T(1,128)S(1)}, s32[1,512]{1,0:T(1,128)}, u32[]{:S(2)}) copy-start(s32[1,512]{1,0:T(1,128)} %refs_17_.1) | copy-start | bytes 6148
  0.0 42.3 %copy-start.2 = (f32[2048]{0:T(1024)S(1)}, f32[2048]{0:T(1024)}, u32[]{:S(2)}) copy-start(f32[2048]{0:T(1024)} %param.25) | copy-start | bytes 24580
  0.0 12.1 %collective-permute-start = (bf16[128,1280]{1,0:T(8,128)(2,1)}, bf16[128,1280]{1,0:T(8,128)(2,1)S(1)}, u32[]{:S(2)}, u32[]{:S(2)}) collective-permute-start(bf16[128,1280]{1,0:T(8,128)(2,1)} %own.1), channel_id=1, source_target_pairs={{0,1},{1,2},{2,3},{3,0},{4,5},{5,6},{6,7},{7,4},{8,9},{9,10},{10,1... | collective-permute-start | bytes 983048 | tf_op jit(solution)/shard_map/ppermute | solution.py:32
  2.1 16.5 %collective-permute-start.1 = (bf16[128,1280]{1,0:T(8,128)(2,1)}, bf16[128,1280]{1,0:T(8,128)(2,1)S(1)}, u32[]{:S(2)}, u32[]{:S(2)}) collective-permute-start(bf16[128,1280]{1,0:T(8,128)(2,1)} %own.1), channel_id=1, source_target_pairs={{0,3},{1,0},{2,1},{3,2},{4,7},{5,4},{6,5},{7,6},{8,11},{9,8},{10,9... | collective-permute-start | bytes 983048 | tf_op jit(solution)/shard_map/ppermute | solution.py:32
  4.3 16.0 %collective-permute-start.2 = (bf16[128,1280]{1,0:T(8,128)(2,1)}, bf16[128,1280]{1,0:T(8,128)(2,1)S(1)}, u32[]{:S(2)}, u32[]{:S(2)}) collective-permute-start(bf16[128,1280]{1,0:T(8,128)(2,1)} %own.1), channel_id=1, source_target_pairs={{0,2},{1,3},{2,0},{3,1},{4,6},{5,7},{6,4},{7,5},{8,10},{9,11},{10,... | collective-permute-start | bytes 983048 | tf_op jit(solution)/shard_map/ppermute | solution.py:32
  7.5 12.9 %copy-start.7 = (bf16[128,128]{0,1:T(8,128)(2,1)}, bf16[128,128]{0,1:T(8,128)(2,1)S(1)}, u32[]{:S(2)}) copy-start(bf16[128,128]{0,1:T(8,128)(2,1)S(1)} %fusion.13) | copy-start | bytes 98308
  9.2 201.2 %copy-start.1 = (s32[4]{0:T(128)}, s32[4]{0:T(128)S(1)}, u32[]{:S(2)}) copy-start(s32[4]{0:T(128)S(1)} %compare_select_fusion.order.refs_0_) | copy-start | bytes 52
  23.7 15.0 %collective-permute-start.3 = (bf16[288,512]{1,0:T(8,128)(2,1)S(1)}, bf16[288,512]{1,0:T(8,128)(2,1)S(1)}, u32[]{:S(2)}, u32[]{:S(2)}) collective-permute-start(bf16[288,512]{1,0:T(8,128)(2,1)S(1)} %get-tuple-element.43.refs_1_.own), channel_id=1, source_target_pairs={{0,1},{1,2},{2,3},{3,0},{4,5},{5,6},{6,7},{7,4},{8,9},{9,10},{10,1... | collective-permute-start | bytes 884744 | tf_op jit(solution)/shard_map/ppermute | solution.py:32
  24.9 17.3 %collective-permute-start.4 = (bf16[288,512]{1,0:T(8,128)(2,1)S(1)}, bf16[288,512]{1,0:T(8,128)(2,1)S(1)}, u32[]{:S(2)}, u32[]{:S(2)}) collective-permute-start(bf16[288,512]{1,0:T(8,128)(2,1)S(1)} %get-tuple-element.43.refs_1_.own), channel_id=1, source_target_pairs={{0,3},{1,0},{2,1},{3,2},{4,7},{5,4},{6,5},{7,6},{8,11},{9,8},{10,9... | collective-permute-start | bytes 884744 | tf_op jit(solution)/shard_map/ppermute | solution.py:32
  27.0 15.3 %collective-permute-start.5 = (bf16[288,512]{1,0:T(8,128)(2,1)S(1)}, bf16[288,512]{1,0:T(8,128)(2,1)S(1)}, u32[]{:S(2)}, u32[]{:S(2)}) collective-permute-start(bf16[288,512]{1,0:T(8,128)(2,1)S(1)} %get-tuple-element.43.refs_1_.own), channel_id=1, source_target_pairs={{0,2},{1,3},{2,0},{3,1},{4,6},{5,7},{6,4},{7,5},{8,10},{9,11},{10,... | collective-permute-start | bytes 884744 | tf_op jit(solution)/shard_map/ppermute | solution.py:32
  38.7 17.2 %collective-permute-start.6 = (bf16[256,512]{1,0:T(8,128)(2,1)S(1)}, bf16[256,512]{1,0:T(8,128)(2,1)S(1)}, u32[]{:S(2)}, u32[]{:S(2)}) collective-permute-start(bf16[256,512]{1,0:T(8,128)(2,1)S(1)} %get-tuple-element.36.refs_1_), channel_id=1, source_target_pairs={{0,1},{1,2},{2,3},{3,0},{4,5},{5,6},{6,7},{7,4},{8,9},{9,10},{10,1... | collective-permute-start | bytes 786440 | tf_op jit(solution)/shard_map/ppermute | solution.py:32
  38.7 18.6 %collective-permute-start.7 = (bf16[256,512]{1,0:T(8,128)(2,1)S(1)}, bf16[256,512]{1,0:T(8,128)(2,1)S(1)}, u32[]{:S(2)}, u32[]{:S(2)}) collective-permute-start(bf16[256,512]{1,0:T(8,128)(2,1)S(1)} %get-tuple-element.36.refs_1_), channel_id=1, source_target_pairs={{0,3},{1,0},{2,1},{3,2},{4,7},{5,4},{6,5},{7,6},{8,11},{9,8},{10,9... | collective-permute-start | bytes 786440 | tf_op jit(solution)/shard_map/ppermute | solution.py:32
  41.9 15.3 %collective-permute-start.8 = (bf16[256,512]{1,0:T(8,128)(2,1)S(1)}, bf16[256,512]{1,0:T(8,128)(2,1)S(1)}, u32[]{:S(2)}, u32[]{:S(2)}) collective-permute-start(bf16[256,512]{1,0:T(8,128)(2,1)S(1)} %get-tuple-element.36.refs_1_), channel_id=1, source_target_pairs={{0,2},{1,3},{2,0},{3,1},{4,6},{5,7},{6,4},{7,5},{8,10},{9,11},{10,... | collective-permute-start | bytes 786440 | tf_op jit(solution)/shard_map/ppermute | solution.py:32
  52.2 21.2 %collective-permute-start.10 = (bf16[256,512]{1,0:T(8,128)(2,1)S(1)}, bf16[256,512]{1,0:T(8,128)(2,1)S(1)}, u32[]{:S(2)}, u32[]{:S(2)}) collective-permute-start(bf16[256,512]{1,0:T(8,128)(2,1)S(1)} %get-tuple-element.49), channel_id=1, source_target_pairs={{0,3},{1,0},{2,1},{3,2},{4,7},{5,4},{6,5},{7,6},{8,11},{9,8},{10,9... | collective-permute-start | bytes 786440 | tf_op jit(solution)/shard_map/ppermute | solution.py:32
  53.9 19.7 %collective-permute-start.11 = (bf16[256,512]{1,0:T(8,128)(2,1)S(1)}, bf16[256,512]{1,0:T(8,128)(2,1)S(1)}, u32[]{:S(2)}, u32[]{:S(2)}) collective-permute-start(bf16[256,512]{1,0:T(8,128)(2,1)S(1)} %get-tuple-element.50), channel_id=1, source_target_pairs={{0,2},{1,3},{2,0},{3,1},{4,6},{5,7},{6,4},{7,5},{8,10},{9,11},{10,... | collective-permute-start | bytes 786440 | tf_op jit(solution)/shard_map/ppermute | solution.py:32
  55.9 17.7 %collective-permute-start.9 = (bf16[256,512]{1,0:T(8,128)(2,1)S(1)}, bf16[256,512]{1,0:T(8,128)(2,1)S(1)}, u32[]{:S(2)}, u32[]{:S(2)}) collective-permute-start(bf16[256,512]{1,0:T(8,128)(2,1)S(1)} %get-tuple-element.48), channel_id=1, source_target_pairs={{0,1},{1,2},{2,3},{3,0},{4,5},{5,6},{6,7},{7,4},{8,9},{9,10},{10,1... | collective-permute-start | bytes 786440 | tf_op jit(solution)/shard_map/ppermute | solution.py:32
  68.0 7.7 %collective-permute-start.12 = (bf16[256,512]{1,0:T(8,128)(2,1)S(1)}, bf16[256,512]{1,0:T(8,128)(2,1)S(1)}, u32[]{:S(2)}, u32[]{:S(2)}) collective-permute-start(bf16[256,512]{1,0:T(8,128)(2,1)S(1)} %get-tuple-element.52), channel_id=1, source_target_pairs={{0,1},{1,2},{2,3},{3,0},{4,5},{5,6},{6,7},{7,4},{8,9},{9,10},{10,1... | collective-permute-start | bytes 786440 | tf_op jit(solution)/shard_map/ppermute | solution.py:32
  68.2 7.4 %collective-permute-start.13 = (bf16[256,512]{1,0:T(8,128)(2,1)S(1)}, bf16[256,512]{1,0:T(8,128)(2,1)S(1)}, u32[]{:S(2)}, u32[]{:S(2)}) collective-permute-start(bf16[256,512]{1,0:T(8,128)(2,1)S(1)} %get-tuple-element.53), channel_id=1, source_target_pairs={{0,3},{1,0},{2,1},{3,2},{4,7},{5,4},{6,5},{7,6},{8,11},{9,8},{10,9... | collective-permute-start | bytes 786440 | tf_op jit(solution)/shard_map/ppermute | solution.py:32
  73.4 12.5 %copy-start.6 = (bf16[128,2,16,512]{3,2,1,0:T(8,128)(2,1)}, bf16[128,2,16,512]{3,2,1,0:T(8,128)(2,1)S(1)}, u32[]{:S(2)}) copy-start(bf16[128,2,16,512]{3,2,1,0:T(8,128)(2,1)S(1)} %get-tuple-element.47) | copy-start | bytes 12582916
  73.4 8.0 %collective-permute-start.14 = (bf16[256,512]{1,0:T(8,128)(2,1)S(1)}, bf16[256,512]{1,0:T(8,128)(2,1)S(1)}, u32[]{:S(2)}, u32[]{:S(2)}) collective-permute-start(bf16[256,512]{1,0:T(8,128)(2,1)S(1)} %get-tuple-element.54), channel_id=1, source_target_pairs={{0,2},{1,3},{2,0},{3,1},{4,6},{5,7},{6,4},{7,5},{8,10},{9,11},{10,... | collective-permute-start | bytes 786440 | tf_op jit(solution)/shard_map/ppermute | solution.py:32
  85.9 60.5 %all-to-all-start.1 = ((bf16[128,32,512]{2,1,0:T(8,128)(2,1)}), bf16[128,32,512]{2,1,0:T(8,128)(2,1)}, u32[]{:S(2)}, u32[]{:S(2)}) async-start(bf16[128,32,512]{2,1,0:T(8,128)(2,1)} %bitcast.65), calls=%async_computation.1 | async-start | bytes 8388608 | tf_op jit(solution)/shard_map/all_to_all | solution.py:409
  146.4 6.0 %copy-start.14 = (f32[2048]{0:T(1024)S(1)}, f32[2048]{0:T(1024)}, u32[]{:S(2)}) copy-start(f32[2048]{0:T(1024)} %param.28) | copy-start | bytes 24580
  146.4 58.2 %all-to-all-start = ((bf16[128,32,512]{2,1,0:T(8,128)(2,1)}), bf16[128,32,512]{2,1,0:T(8,128)(2,1)}, u32[]{:S(2)}, u32[]{:S(2)}) async-start(bf16[128,32,512]{2,1,0:T(8,128)(2,1)} %bitcast.64), calls=%async_computation | async-start | bytes 8388608 | tf_op jit(solution)/shard_map/all_to_all | solution.py:409
  204.6 59.5 %all-to-all-start.2 = ((bf16[128,8,2048]{2,1,0:T(8,128)(2,1)}), bf16[128,8,2048]{2,1,0:T(8,128)(2,1)}, u32[]{:S(2)}, u32[]{:S(2)}) async-start(bf16[128,8,2048]{2,1,0:T(8,128)(2,1)} %bitcast.62), calls=%async_computation.2 | async-start | bytes 8388608 | tf_op jit(solution)/shard_map/all_to_all | solution.py:409
  219.3 41.0 %collective-permute-start.15 = (bf16[128,512]{1,0:T(8,128)(2,1)S(1)}, bf16[128,512]{1,0:T(8,128)(2,1)S(1)}, u32[]{:S(2)}, u32[]{:S(2)}) collective-permute-start(bf16[128,512]{1,0:T(8,128)(2,1)S(1)} %get-tuple-element.65), channel_id=1, source_target_pairs={{0,1},{1,2},{2,3},{3,0},{4,5},{5,6},{6,7},{7,4},{8,9},{9,10},{10,1... | collective-permute-start | bytes 393224 | tf_op jit(solution)/shard_map/ppermute | solution.py:32
  220.3 40.0 %collective-permute-start.16 = (bf16[128,512]{1,0:T(8,128)(2,1)S(1)}, bf16[128,512]{1,0:T(8,128)(2,1)S(1)}, u32[]{:S(2)}, u32[]{:S(2)}) collective-permute-start(bf16[128,512]{1,0:T(8,128)(2,1)S(1)} %get-tuple-element.64), channel_id=1, source_target_pairs={{0,3},{1,0},{2,1},{3,2},{4,7},{5,4},{6,5},{7,6},{8,11},{9,8},{10,9... | collective-permute-start | bytes 393224 | tf_op jit(solution)/shard_map/ppermute | solution.py:32
  222.5 41.5 %collective-permute-start.17 = (bf16[128,512]{1,0:T(8,128)(2,1)S(1)}, bf16[128,512]{1,0:T(8,128)(2,1)S(1)}, u32[]{:S(2)}, u32[]{:S(2)}) collective-permute-start(bf16[128,512]{1,0:T(8,128)(2,1)S(1)} %get-tuple-element.63), channel_id=1, source_target_pairs={{0,2},{1,3},{2,0},{3,1},{4,6},{5,7},{6,4},{7,5},{8,10},{9,11},{10,... | collective-permute-start | bytes 393224 | tf_op jit(solution)/shard_map/ppermute | solution.py:32
  260.3 3.8 %copy-start.10 = (bf16[128,512]{1,0:T(8,128)(2,1)}, bf16[128,512]{1,0:T(8,128)(2,1)S(1)}, u32[]{:S(2)}) copy-start(bf16[128,512]{1,0:T(8,128)(2,1)S(1)} %collective-permute-done.16.right) | copy-start | bytes 393220
  264.1 9.6 %copy-start.8 = (bf16[128,128]{0,1:T(8,128)(2,1)S(1)}, bf16[128,128]{0,1:T(8,128)(2,1)}, u32[]{:S(2)}) copy-start(bf16[128,128]{0,1:T(8,128)(2,1)} %copy-done.7) | copy-start | bytes 98308
  264.1 13.0 %copy-start.13 = (pred[128,128]{0,1:T(32,128)(4,1)S(1)}, pred[128,128]{0,1:T(32,128)(4,1)}, u32[]{:S(2)}) copy-start(pred[128,128]{0,1:T(32,128)(4,1)} %copy-done.12) | copy-start | bytes 49156
  264.7 61.1 %all-to-all-start.3 = ((bf16[128,8,2048]{2,1,0:T(8,128)(2,1)}), bf16[128,8,2048]{2,1,0:T(8,128)(2,1)}, u32[]{:S(2)}, u32[]{:S(2)}) async-start(bf16[128,8,2048]{2,1,0:T(8,128)(2,1)} %bitcast.63), calls=%async_computation.3 | async-start | bytes 8388608 | tf_op jit(solution)/shard_map/all_to_all | solution.py:409
  (5 other events, 6.3 us)
where the time goes:
time: 331 us; the launch traced here: 330 us
  waiting for transfers between devices  177 us (53%)
  Pallas kernels  59.6 us (18%)
  starting transfers between devices  55.3 us (17%)
  matrix products  19.8 us (6%)
  between operations  7.77 us (2%)
  local copies, waits for them, and re-layouts  6.07 us (2%)
  other arithmetic  3.8 us (1%)
    all_to_all x4, waiting for transfers between devices, travel(): return lax.all_to_all(rows, ('exp', 'tp'), 0, 0, tiled=True)  125 us
    ppermute x18, waiting for transfers between devices, shift(): lax.ppermute(value, 'tp', [(i, (i + by) % size) for i in range(size)])  52.7 us
    pallas_call x2, Pallas kernels, run_experts(): pl.pallas_call(expert_kernel, grid=(sources // groups,), in_specs=[pl.Blo...  32.9 us
    all_to_all x4, starting transfers between devices, travel(): return lax.all_to_all(rows, ('exp', 'tp'), 0, 0, tiled=True)  29.1 us
    ppermute x18, starting transfers between devices, shift(): lax.ppermute(value, 'tp', [(i, (i + by) % size) for i in range(size)])  26.1 us
    pallas_call x2, Pallas kernels, run_layer(): pl.pallas_call(kernel, in_specs=[pl.BlockSpec(memory_space=pltpu.SMEM)] +...  19.3 us
    dot_general x2, matrix products, on_device(): jnp.dot(chosen.reshape(-1, seq_len), blocks, preferred_element_type=F32)  10.8 us
    dot_general x2, matrix products, on_device(): total = total + jnp.dot(combine, returned[part], preferred_element_type=F32)  6.77 us
  transfers between devices with their start and end apart: 22, of which 11 were waited for; matrix products, arithmetic and copies ran while one was open for 6% of the time, Pallas kernels for 17%

commit v1 on v0

--- a/solution.py
+++ b/solution.py
@@ -55,10 +55,13 @@
     first[pl.ds(some * rows, extra.shape[0]), :] = extra[...]
     part = bias[pl.ds(order[0], 1), :]
     last.wait()
-    for place, copy in enumerate(copies):
-        copy.wait()
-        product = jnp.dot(near[place], weight[...], preferred_element_type=F32)
-        product = (product + part).astype(BF16)
+    for copy in copies:
+        copy.wait()
+    frames = near[...].reshape(-1, near.shape[-1])
+    columns = jnp.dot(frames, weight[...], preferred_element_type=F32)
+    columns = (columns + part).astype(BF16)
+    for place in range(len(copies)):
+        product = columns[place * rows : (place + 1) * rows]
         at = order[place]
         for number in range(2 * some):
             out = (first, second)[number // some]
@@ -156,13 +159,21 @@
     copies = [
         pltpu.make_async_copy(source.at[pl.ds(0, count), :], near.at[place], sems.at[place])
         for place, source in enumerate(sources)
-    ] + [
-        pltpu.make_async_copy(source, target, sems.at[4 + place])
-        for place, (source, target) in enumerate(zip(weights, (w_k, w_v, w_q, w_o)))
     ]
+    split = {}
+    for place, (source, target) in enumerate(zip(weights, (w_k, w_v, w_q, w_o))):
+        count_of = 1 if place < 2 else 4
+        depth = target.shape[0] // count_of
+        split[place] = [
+            pltpu.make_async_copy(
+                source.at[pl.ds(part * depth, depth), :], target.at[pl.ds(part * depth, depth), :],
+                sems.at[4 + 4 * place + part],
+            )
+            for part in range(count_of)
+        ]
+    for copy in copies + split[0] + split[1] + split[2] + split[3]:
+        copy.start()
     for copy in copies:
-        copy.start()
-    for copy in copies[:4]:
         copy.wait()
 
     pieces = [near[place].astype(F32) for place in range(4)]
@@ -184,15 +195,18 @@
     if first:
         keys[:first, :] = past_keys[...]
         values[:first, :] = past_values[...]
-    copies[4].wait()
+    for copy in split[0]:
+        copy.wait()
     new_keys = head_of(jnp.dot(normed[...], w_k[...], preferred_element_type=F32), k_gain)
-    copies[5].wait()
+    for copy in split[1]:
+        copy.wait()
     new_values = jnp.dot(normed[...], w_v[...], preferred_element_type=F32).astype(BF16)
     keys[here, :] = new_keys
     values[here, :] = new_values
     keys_out[...] = new_keys
     values_out[...] = new_values
-    copies[6].wait()
+    for copy in split[2]:
+        copy.wait()
     for pair in range(heads // 2):
         raw = jnp.dot(
             normed[...], w_q[:, pl.ds(pair * 2 * head_dim, 2 * head_dim)],
@@ -220,7 +234,8 @@
                 mixed / total
             ).astype(BF16)
 
-    copies[7].wait()
+    for copy in split[3]:
+        copy.wait()
     for place, out in ((2, to_right), (1, to_left), (3, to_opposite), (0, to_own)):
         columns = pl.ds(pl.multiple_of(order[place] * width, width), width)
         out[...] = jnp.dot(context[...], w_o[:, columns], preferred_element_type=F32).astype(BF16)
@@ -258,7 +273,7 @@
             pltpu.VMEM((len(parts), count, width), BF16),
         ]
         + [pltpu.VMEM(weight.shape, BF16) for weight in weights]
-        + [pltpu.SemaphoreType.DMA((len(parts) + len(weights),))],
+        + [pltpu.SemaphoreType.DMA((len(parts) + 4 * len(weights),))],
         compiler_params=pltpu.CompilerParams(vmem_limit_bytes=VMEM_BYTES),
         cost_estimate=pl.CostEstimate(
             flops=4 * count * feat_dim * (heads + 1) * head_dim

time: 331 us -> 331 us (level)
  no operation moved by 1% of the time
where the time goes in v1:
time: 331 us; the launch traced here: 329 us
  waiting for transfers between devices  177 us (53%)
  Pallas kernels  59.3 us (18%)
  starting transfers between devices  55.3 us (17%)
  matrix products  19.8 us (6%)
  between operations  7.78 us (2%)
  local copies, waits for them, and re-layouts  6.07 us (2%)
  other arithmetic  3.8 us (1%)
    all_to_all x4, waiting for transfers between devices, travel(): return lax.all_to_all(rows, ('exp', 'tp'), 0, 0, tiled=True)  125 us
    ppermute x18, waiting for transfers between devices, shift(): lax.ppermute(value, 'tp', [(i, (i + by) % size) for i in range(size)])  52.7 us
    pallas_call x2, Pallas kernels, run_experts(): pl.pallas_call(expert_kernel, grid=(sources // groups,), in_specs=[pl.Blo...  32.9 us
    all_to_all x4, starting transfers between devices, travel(): return lax.all_to_all(rows, ('exp', 'tp'), 0, 0, tiled=True)  29.1 us
    ppermute x18, starting transfers between devices, shift(): lax.ppermute(value, 'tp', [(i, (i + by) % size) for i in range(size)])  26.1 us
    pallas_call x2, Pallas kernels, run_layer(): pl.pallas_call(kernel, in_specs=[pl.BlockSpec(memory_space=pltpu.SMEM)] +...  19.5 us
    dot_general x2, matrix products, on_device(): jnp.dot(chosen.reshape(-1, seq_len), blocks, preferred_element_type=F32)  10.8 us
    dot_general x2, matrix products, on_device(): total = total + jnp.dot(combine, returned[part], preferred_element_type=F32)  6.77 us
  transfers between devices with their start and end apart: 22, of which 11 were waited for; matrix products, arithmetic and copies ran while one was open for 6% of the time, Pallas kernels for 17%

profile of v1, /device:TPU:0, one launch (start us, length us, event | category | flops | bytes accessed | tf_op | source)
XLA Modules:
  0.0 329.3 jit_solution(4311723895347624394)
XLA Ops:
  0.0 2.1 collective-permute-start
  2.1 2.2 collective-permute-start.1
  9.2 2.9 collective-permute-done.left
  12.1 6.5 %collective-permute-done.1.right = bf16[128,1280]{1,0:T(8,128)(2,1)S(1)} collective-permute-done((bf16[128,1280]{1,0:T(8,128)(2,1)}, bf16[128,1280]{1,0:T(8,128)(2,1)S(1)}, u32[]{:S(2)}, u32[]{:S(2)}) %collective-permute-start.1) | collective-permute-done | bytes 327712 | tf_op jit(solution)/shard_map/ppermute | solution.py:32
  20.3 2.9 columns.1
  24.5 2.1 collective-permute-start.4
  27.7 10.5 %collective-permute-done.3.refs_2_.left = bf16[288,512]{1,0:T(8,128)(2,1)S(1)} collective-permute-done((bf16[288,512]{1,0:T(8,128)(2,1)S(1)}, bf16[288,512]{1,0:T(8,128)(2,1)S(1)}, u32[]{:S(2)}, u32[]{:S(2)}) %collective-permute-start.3) | collective-permute-done | bytes 294944 | tf_op jit(solution)/shard_map/ppermute | solution.py:32
  38.2 3.2 collective-permute-start.7
  43.2 8.7 %layer.2 = (bf16[256,512]{1,0:T(8,128)(2,1)S(1)}, bf16[256,512]{1,0:T(8,128)(2,1)S(1)}, bf16[256,512]{1,0:T(8,128)(2,1)S(1)}, bf16[256,512]{1,0:T(8,128)(2,1)S(1...) custom-call(s32[4]{0:T(128)S(1)} %compare_select_fusion.order.refs_0_, ...), custom_call_target="tpu_custom_call" | custom-call | flops 2684354560 | bytes 11534336 | tf_op jit(solution)/shard_map/layer/pallas_call | solution.py:260
  53.5 2.0 collective-permute-start.11
  56.8 10.8 %layer.3 = (bf16[256,512]{1,0:T(8,128)(2,1)S(1)}, bf16[256,512]{1,0:T(8,128)(2,1)S(1)}, bf16[256,512]{1,0:T(8,128)(2,1)S(1)}, bf16[256,512]{1,0:T(8,128)(2,1)S(1...) custom-call(s32[4]{0:T(128)S(1)} %compare_select_fusion.order.refs_0_, ...), custom_call_target="tpu_custom_call" | custom-call | flops 2952790016 | bytes 11534336 | tf_op jit(solution)/shard_map/layer/pallas_call | solution.py:260
  67.9 3.1 collective-permute-start.13
  71.0 2.1 chosen.1
  73.5 1.8 collective-permute-done.12
  75.3 5.7 %collective-permute-done.14 = bf16[256,512]{1,0:T(8,128)(2,1)S(1)} collective-permute-done((bf16[256,512]{1,0:T(8,128)(2,1)S(1)}, bf16[256,512]{1,0:T(8,128)(2,1)S(1)}, u32[]{:S(2)}, u32[]{:S(2)}) %collective-permute-start.14) | collective-permute-done | bytes 262176 | tf_op jit(solution)/shard_map/ppermute | solution.py:32
  81.2 4.4 %convolution_convert_fusion = bf16[4096,512]{1,0:T(8,128)(2,1)} fusion(bf16[4096,512]{1,0:T(8,128)(2,1)S(1)} %bitcast.61, bf16[256,512]{1,0:T(8,128)(2,1)S(1)} %add_convert_fusion, bf16[256,512]{1,0:T(8,128)(2,1)S(1)} %add_convert_fusion.1), kind=kOutput, calls=%fused_computation | convolution fusion | flops 2150629376 | bytes 8912896 | tf_op jit(solution)/shard_map/dot_general | solution.py:428
  85.6 8.5 %all-to-all-start.1 = ((bf16[128,32,512]{2,1,0:T(8,128)(2,1)}), bf16[128,32,512]{2,1,0:T(8,128)(2,1)}, u32[]{:S(2)}, u32[]{:S(2)}) async-start(bf16[128,32,512]{2,1,0:T(8,128)(2,1)} %bitcast.65), calls=%async_computation.1 | async-start | bytes 8388608 | tf_op jit(solution)/shard_map/all_to_all | solution.py:424
  94.0 6.4 %convolution_convert_fusion.1 = bf16[4096,512]{1,0:T(8,128)(2,1)} fusion(bf16[4096,512]{1,0:T(8,128)(2,1)} %bitcast.60, bf16[256,512]{1,0:T(8,128)(2,1)S(1)} %add_convert_fusion, bf16[256,512]{1,0:T(8,128)(2,1)S(1)} %add_convert_fusion.1), kind=kOutput, calls=%fused_computation.1 | convolution fusion | flops 2150629376 | bytes 8912896 | tf_op jit(solution)/shard_map/dot_general | solution.py:428
  100.5 45.6 %all-to-all-done.1 = bf16[128,32,512]{2,1,0:T(8,128)(2,1)} async-done(((bf16[128,32,512]{2,1,0:T(8,128)(2,1)}), bf16[128,32,512]{2,1,0:T(8,128)(2,1)}, u32[]{:S(2)}, u32[]{:S(2)}) %all-to-all-start.1) | async-done | bytes 4194336 | tf_op jit(solution)/shard_map/all_to_all | solution.py:424
  146.1 6.0 %all-to-all-start = ((bf16[128,32,512]{2,1,0:T(8,128)(2,1)}), bf16[128,32,512]{2,1,0:T(8,128)(2,1)}, u32[]{:S(2)}, u32[]{:S(2)}) async-start(bf16[128,32,512]{2,1,0:T(8,128)(2,1)} %bitcast.64), calls=%async_computation | async-start | bytes 8388608 | tf_op jit(solution)/shard_map/all_to_all | solution.py:424
  152.7 16.5 %experts.3 = bf16[1024,2048]{1,0:T(8,128)(2,1)} custom-call(bf16[32,4,32,512]{3,2,1,0:T(8,128)(2,1)} %bitcast.15.rows, f32[4,512]{1,0:T(4,128)} %reshape.102.gain, bf16[2048,1536]{1,0:T(8,128)(2,1)} %bitcast.69, bf16[768,2048]{1,0:T(8,128)(2,1)} %bitcast.71), custom_call_target="tpu_custom_call" | custom-call | flops 9663676416 | bytes 17825792 | tf_op jit(solution)/shard_map/experts/pallas_call | solution.py:315
  169.2 35.1 %all-to-all-done = bf16[128,32,512]{2,1,0:T(8,128)(2,1)} async-done(((bf16[128,32,512]{2,1,0:T(8,128)(2,1)}), bf16[128,32,512]{2,1,0:T(8,128)(2,1)}, u32[]{:S(2)}, u32[]{:S(2)}) %all-to-all-start) | async-done | bytes 4194336 | tf_op jit(solution)/shard_map/all_to_all | solution.py:424
  204.3 5.8 %all-to-all-start.2 = ((bf16[128,8,2048]{2,1,0:T(8,128)(2,1)}), bf16[128,8,2048]{2,1,0:T(8,128)(2,1)}, u32[]{:S(2)}, u32[]{:S(2)}) async-start(bf16[128,8,2048]{2,1,0:T(8,128)(2,1)} %bitcast.62), calls=%async_computation.2 | async-start | bytes 8388608 | tf_op jit(solution)/shard_map/all_to_all | solution.py:424
  220.0 2.2 collective-permute-start.16
  223.8 16.4 %experts.2 = bf16[1024,2048]{1,0:T(8,128)(2,1)} custom-call(bf16[32,4,32,512]{3,2,1,0:T(8,128)(2,1)} %bitcast.9.rows, f32[4,512]{1,0:T(4,128)} %reshape.102.gain, bf16[2048,1536]{1,0:T(8,128)(2,1)} %bitcast.70, bf16[768,2048]{1,0:T(8,128)(2,1)} %bitcast.72), custom_call_target="tpu_custom_call" | custom-call | flops 9663676416 | bytes 17825792 | tf_op jit(solution)/shard_map/experts/pallas_call | solution.py:315
  240.2 19.8 %collective-permute-done.15.left = bf16[128,512]{1,0:T(8,128)(2,1)S(1)} collective-permute-done((bf16[128,512]{1,0:T(8,128)(2,1)S(1)}, bf16[128,512]{1,0:T(8,128)(2,1)S(1)}, u32[]{:S(2)}, u32[]{:S(2)}) %collective-permute-start.15) | collective-permute-done | bytes 131104 | tf_op jit(solution)/shard_map/ppermute | solution.py:32
  260.0 3.7 %collective-permute-done.17.opposite = bf16[128,512]{1,0:T(8,128)(2,1)S(1)} collective-permute-done((bf16[128,512]{1,0:T(8,128)(2,1)S(1)}, bf16[128,512]{1,0:T(8,128)(2,1)S(1)}, u32[]{:S(2)}, u32[]{:S(2)}) %collective-permute-start.17) | collective-permute-done | bytes 131104 | tf_op jit(solution)/shard_map/ppermute | solution.py:32
  264.4 8.9 %all-to-all-start.3 = ((bf16[128,8,2048]{2,1,0:T(8,128)(2,1)}), bf16[128,8,2048]{2,1,0:T(8,128)(2,1)}, u32[]{:S(2)}, u32[]{:S(2)}) async-start(bf16[128,8,2048]{2,1,0:T(8,128)(2,1)} %bitcast.63), calls=%async_computation.3 | async-start | bytes 8388608 | tf_op jit(solution)/shard_map/all_to_all | solution.py:424
  273.6 1.9 join.1
  278.6 3.0 fusion.4
  281.6 43.9 %all-to-all-done.3 = bf16[128,8,2048]{2,1,0:T(8,128)(2,1)} async-done(((bf16[128,8,2048]{2,1,0:T(8,128)(2,1)}), bf16[128,8,2048]{2,1,0:T(8,128)(2,1)}, u32[]{:S(2)}, u32[]{:S(2)}) %all-to-all-start.3) | async-done | bytes 4194336 | tf_op jit(solution)/shard_map/all_to_all | solution.py:424
  325.6 3.7 %fusion.10 = bf16[128,2048]{1,0:T(8,128)(2,1)} fusion(f32[128,2048]{1,0:T(8,128)S(1)} %fusion.4, bf16[128,8,2048]{2,1,0:T(8,128)(2,1)} %all-to-all-done.3, bf16[128,1024]{1,0:T(8,128)(2,1)S(1)} %fusion.21, f32[128,1024]{1,0:T(8,128)S(1)} %fusion.22, f32[1024]{0:T(1024)S(1)} %fusion.45), kind=kOutput, calls=%fused_computation.8 | convolution fusion | flops 537657344 | bytes 6557696 | tf_op jit(solution)/shard_map/dot_general | solution.py:464
  (80 shorter events, 23.0 us)
Async XLA Ops:
  0.0 276.8 %copy-start = (bf16[2048,128]{1,0:T(8,128)(2,1)S(1)}, bf16[2048,128]{1,0:T(8,128)(2,1)}, u32[]{:S(2)}) copy-start(bf16[2048,128]{1,0:T(8,128)(2,1)} %param.29) | copy-start | bytes 1572868
  0.0 41.6 %copy-start.3 = (s32[1,512]{1,0:T(1,128)S(1)}, s32[1,512]{1,0:T(1,128)}, u32[]{:S(2)}) copy-start(s32[1,512]{1,0:T(1,128)} %refs_17_.1) | copy-start | bytes 6148
  0.0 41.8 %copy-start.2 = (f32[2048]{0:T(1024)S(1)}, f32[2048]{0:T(1024)}, u32[]{:S(2)}) copy-start(f32[2048]{0:T(1024)} %param.25) | copy-start | bytes 24580
  0.0 12.1 %collective-permute-start = (bf16[128,1280]{1,0:T(8,128)(2,1)}, bf16[128,1280]{1,0:T(8,128)(2,1)S(1)}, u32[]{:S(2)}, u32[]{:S(2)}) collective-permute-start(bf16[128,1280]{1,0:T(8,128)(2,1)} %own.1), channel_id=1, source_target_pairs={{0,1},{1,2},{2,3},{3,0},{4,5},{5,6},{6,7},{7,4},{8,9},{9,10},{10,1... | collective-permute-start | bytes 983048 | tf_op jit(solution)/shard_map/ppermute | solution.py:32
  2.1 16.5 %collective-permute-start.1 = (bf16[128,1280]{1,0:T(8,128)(2,1)}, bf16[128,1280]{1,0:T(8,128)(2,1)S(1)}, u32[]{:S(2)}, u32[]{:S(2)}) collective-permute-start(bf16[128,1280]{1,0:T(8,128)(2,1)} %own.1), channel_id=1, source_target_pairs={{0,3},{1,0},{2,1},{3,2},{4,7},{5,4},{6,5},{7,6},{8,11},{9,8},{10,9... | collective-permute-start | bytes 983048 | tf_op jit(solution)/shard_map/ppermute | solution.py:32
  4.3 16.0 %collective-permute-start.2 = (bf16[128,1280]{1,0:T(8,128)(2,1)}, bf16[128,1280]{1,0:T(8,128)(2,1)S(1)}, u32[]{:S(2)}, u32[]{:S(2)}) collective-permute-start(bf16[128,1280]{1,0:T(8,128)(2,1)} %own.1), channel_id=1, source_target_pairs={{0,2},{1,3},{2,0},{3,1},{4,6},{5,7},{6,4},{7,5},{8,10},{9,11},{10,... | collective-permute-start | bytes 983048 | tf_op jit(solution)/shard_map/ppermute | solution.py:32
  7.5 12.9 %copy-start.7 = (bf16[128,128]{0,1:T(8,128)(2,1)}, bf16[128,128]{0,1:T(8,128)(2,1)S(1)}, u32[]{:S(2)}) copy-start(bf16[128,128]{0,1:T(8,128)(2,1)S(1)} %fusion.13) | copy-start | bytes 98308
  9.2 200.9 %copy-start.1 = (s32[4]{0:T(128)}, s32[4]{0:T(128)S(1)}, u32[]{:S(2)}) copy-start(s32[4]{0:T(128)S(1)} %compare_select_fusion.order.refs_0_) | copy-start | bytes 52
  23.2 14.9 %collective-permute-start.3 = (bf16[288,512]{1,0:T(8,128)(2,1)S(1)}, bf16[288,512]{1,0:T(8,128)(2,1)S(1)}, u32[]{:S(2)}, u32[]{:S(2)}) collective-permute-start(bf16[288,512]{1,0:T(8,128)(2,1)S(1)} %get-tuple-element.43.refs_1_.own), channel_id=1, source_target_pairs={{0,1},{1,2},{2,3},{3,0},{4,5},{5,6},{6,7},{7,4},{8,9},{9,10},{10,1... | collective-permute-start | bytes 884744 | tf_op jit(solution)/shard_map/ppermute | solution.py:32
  24.5 17.3 %collective-permute-start.4 = (bf16[288,512]{1,0:T(8,128)(2,1)S(1)}, bf16[288,512]{1,0:T(8,128)(2,1)S(1)}, u32[]{:S(2)}, u32[]{:S(2)}) collective-permute-start(bf16[288,512]{1,0:T(8,128)(2,1)S(1)} %get-tuple-element.43.refs_1_.own), channel_id=1, source_target_pairs={{0,3},{1,0},{2,1},{3,2},{4,7},{5,4},{6,5},{7,6},{8,11},{9,8},{10,9... | collective-permute-start | bytes 884744 | tf_op jit(solution)/shard_map/ppermute | solution.py:32
  26.6 15.3 %collective-permute-start.5 = (bf16[288,512]{1,0:T(8,128)(2,1)S(1)}, bf16[288,512]{1,0:T(8,128)(2,1)S(1)}, u32[]{:S(2)}, u32[]{:S(2)}) collective-permute-start(bf16[288,512]{1,0:T(8,128)(2,1)S(1)} %get-tuple-element.43.refs_1_.own), channel_id=1, source_target_pairs={{0,2},{1,3},{2,0},{3,1},{4,6},{5,7},{6,4},{7,5},{8,10},{9,11},{10,... | collective-permute-start | bytes 884744 | tf_op jit(solution)/shard_map/ppermute | solution.py:32
  38.2 17.3 %collective-permute-start.6 = (bf16[256,512]{1,0:T(8,128)(2,1)S(1)}, bf16[256,512]{1,0:T(8,128)(2,1)S(1)}, u32[]{:S(2)}, u32[]{:S(2)}) collective-permute-start(bf16[256,512]{1,0:T(8,128)(2,1)S(1)} %get-tuple-element.36.refs_1_), channel_id=1, source_target_pairs={{0,1},{1,2},{2,3},{3,0},{4,5},{5,6},{6,7},{7,4},{8,9},{9,10},{10,1... | collective-permute-start | bytes 786440 | tf_op jit(solution)/shard_map/ppermute | solution.py:32
  38.2 18.6 %collective-permute-start.7 = (bf16[256,512]{1,0:T(8,128)(2,1)S(1)}, bf16[256,512]{1,0:T(8,128)(2,1)S(1)}, u32[]{:S(2)}, u32[]{:S(2)}) collective-permute-start(bf16[256,512]{1,0:T(8,128)(2,1)S(1)} %get-tuple-element.36.refs_1_), channel_id=1, source_target_pairs={{0,3},{1,0},{2,1},{3,2},{4,7},{5,4},{6,5},{7,6},{8,11},{9,8},{10,9... | collective-permute-start | bytes 786440 | tf_op jit(solution)/shard_map/ppermute | solution.py:32
  41.4 15.4 %collective-permute-start.8 = (bf16[256,512]{1,0:T(8,128)(2,1)S(1)}, bf16[256,512]{1,0:T(8,128)(2,1)S(1)}, u32[]{:S(2)}, u32[]{:S(2)}) collective-permute-start(bf16[256,512]{1,0:T(8,128)(2,1)S(1)} %get-tuple-element.36.refs_1_), channel_id=1, source_target_pairs={{0,2},{1,3},{2,0},{3,1},{4,6},{5,7},{6,4},{7,5},{8,10},{9,11},{10,... | collective-permute-start | bytes 786440 | tf_op jit(solution)/shard_map/ppermute | solution.py:32
  51.8 21.3 %collective-permute-start.10 = (bf16[256,512]{1,0:T(8,128)(2,1)S(1)}, bf16[256,512]{1,0:T(8,128)(2,1)S(1)}, u32[]{:S(2)}, u32[]{:S(2)}) collective-permute-start(bf16[256,512]{1,0:T(8,128)(2,1)S(1)} %get-tuple-element.49), channel_id=1, source_target_pairs={{0,3},{1,0},{2,1},{3,2},{4,7},{5,4},{6,5},{7,6},{8,11},{9,8},{10,9... | collective-permute-start | bytes 786440 | tf_op jit(solution)/shard_map/ppermute | solution.py:32
  53.5 19.8 %collective-permute-start.11 = (bf16[256,512]{1,0:T(8,128)(2,1)S(1)}, bf16[256,512]{1,0:T(8,128)(2,1)S(1)}, u32[]{:S(2)}, u32[]{:S(2)}) collective-permute-start(bf16[256,512]{1,0:T(8,128)(2,1)S(1)} %get-tuple-element.50), channel_id=1, source_target_pairs={{0,2},{1,3},{2,0},{3,1},{4,6},{5,7},{6,4},{7,5},{8,10},{9,11},{10,... | collective-permute-start | bytes 786440 | tf_op jit(solution)/shard_map/ppermute | solution.py:32
  55.5 17.8 %collective-permute-start.9 = (bf16[256,512]{1,0:T(8,128)(2,1)S(1)}, bf16[256,512]{1,0:T(8,128)(2,1)S(1)}, u32[]{:S(2)}, u32[]{:S(2)}) collective-permute-start(bf16[256,512]{1,0:T(8,128)(2,1)S(1)} %get-tuple-element.48), channel_id=1, source_target_pairs={{0,1},{1,2},{2,3},{3,0},{4,5},{5,6},{6,7},{7,4},{8,9},{9,10},{10,1... | collective-permute-start | bytes 786440 | tf_op jit(solution)/shard_map/ppermute | solution.py:32
  67.7 7.7 %collective-permute-start.12 = (bf16[256,512]{1,0:T(8,128)(2,1)S(1)}, bf16[256,512]{1,0:T(8,128)(2,1)S(1)}, u32[]{:S(2)}, u32[]{:S(2)}) collective-permute-start(bf16[256,512]{1,0:T(8,128)(2,1)S(1)} %get-tuple-element.52), channel_id=1, source_target_pairs={{0,1},{1,2},{2,3},{3,0},{4,5},{5,6},{6,7},{7,4},{8,9},{9,10},{10,1... | collective-permute-start | bytes 786440 | tf_op jit(solution)/shard_map/ppermute | solution.py:32
  67.9 7.4 %collective-permute-start.13 = (bf16[256,512]{1,0:T(8,128)(2,1)S(1)}, bf16[256,512]{1,0:T(8,128)(2,1)S(1)}, u32[]{:S(2)}, u32[]{:S(2)}) collective-permute-start(bf16[256,512]{1,0:T(8,128)(2,1)S(1)} %get-tuple-element.53), channel_id=1, source_target_pairs={{0,3},{1,0},{2,1},{3,2},{4,7},{5,4},{6,5},{7,6},{8,11},{9,8},{10,9... | collective-permute-start | bytes 786440 | tf_op jit(solution)/shard_map/ppermute | solution.py:32
  73.1 12.5 %copy-start.6 = (bf16[128,2,16,512]{3,2,1,0:T(8,128)(2,1)}, bf16[128,2,16,512]{3,2,1,0:T(8,128)(2,1)S(1)}, u32[]{:S(2)}) copy-start(bf16[128,2,16,512]{3,2,1,0:T(8,128)(2,1)S(1)} %get-tuple-element.47) | copy-start | bytes 12582916
  73.1 8.0 %collective-permute-start.14 = (bf16[256,512]{1,0:T(8,128)(2,1)S(1)}, bf16[256,512]{1,0:T(8,128)(2,1)S(1)}, u32[]{:S(2)}, u32[]{:S(2)}) collective-permute-start(bf16[256,512]{1,0:T(8,128)(2,1)S(1)} %get-tuple-element.54), channel_id=1, source_target_pairs={{0,2},{1,3},{2,0},{3,1},{4,6},{5,7},{6,4},{7,5},{8,10},{9,11},{10,... | collective-permute-start | bytes 786440 | tf_op jit(solution)/shard_map/ppermute | solution.py:32
  85.6 60.5 %all-to-all-start.1 = ((bf16[128,32,512]{2,1,0:T(8,128)(2,1)}), bf16[128,32,512]{2,1,0:T(8,128)(2,1)}, u32[]{:S(2)}, u32[]{:S(2)}) async-start(bf16[128,32,512]{2,1,0:T(8,128)(2,1)} %bitcast.65), calls=%async_computation.1 | async-start | bytes 8388608 | tf_op jit(solution)/shard_map/all_to_all | solution.py:424
  146.1 6.0 %copy-start.14 = (f32[2048]{0:T(1024)S(1)}, f32[2048]{0:T(1024)}, u32[]{:S(2)}) copy-start(f32[2048]{0:T(1024)} %param.28) | copy-start | bytes 24580
  146.1 58.2 %all-to-all-start = ((bf16[128,32,512]{2,1,0:T(8,128)(2,1)}), bf16[128,32,512]{2,1,0:T(8,128)(2,1)}, u32[]{:S(2)}, u32[]{:S(2)}) async-start(bf16[128,32,512]{2,1,0:T(8,128)(2,1)} %bitcast.64), calls=%async_computation | async-start | bytes 8388608 | tf_op jit(solution)/shard_map/all_to_all | solution.py:424
  204.3 59.5 %all-to-all-start.2 = ((bf16[128,8,2048]{2,1,0:T(8,128)(2,1)}), bf16[128,8,2048]{2,1,0:T(8,128)(2,1)}, u32[]{:S(2)}, u32[]{:S(2)}) async-start(bf16[128,8,2048]{2,1,0:T(8,128)(2,1)} %bitcast.62), calls=%async_computation.2 | async-start | bytes 8388608 | tf_op jit(solution)/shard_map/all_to_all | solution.py:424
  219.0 41.0 %collective-permute-start.15 = (bf16[128,512]{1,0:T(8,128)(2,1)S(1)}, bf16[128,512]{1,0:T(8,128)(2,1)S(1)}, u32[]{:S(2)}, u32[]{:S(2)}) collective-permute-start(bf16[128,512]{1,0:T(8,128)(2,1)S(1)} %get-tuple-element.65), channel_id=1, source_target_pairs={{0,1},{1,2},{2,3},{3,0},{4,5},{5,6},{6,7},{7,4},{8,9},{9,10},{10,1... | collective-permute-start | bytes 393224 | tf_op jit(solution)/shard_map/ppermute | solution.py:32
  220.0 40.0 %collective-permute-start.16 = (bf16[128,512]{1,0:T(8,128)(2,1)S(1)}, bf16[128,512]{1,0:T(8,128)(2,1)S(1)}, u32[]{:S(2)}, u32[]{:S(2)}) collective-permute-start(bf16[128,512]{1,0:T(8,128)(2,1)S(1)} %get-tuple-element.64), channel_id=1, source_target_pairs={{0,3},{1,0},{2,1},{3,2},{4,7},{5,4},{6,5},{7,6},{8,11},{9,8},{10,9... | collective-permute-start | bytes 393224 | tf_op jit(solution)/shard_map/ppermute | solution.py:32
  222.2 41.5 %collective-permute-start.17 = (bf16[128,512]{1,0:T(8,128)(2,1)S(1)}, bf16[128,512]{1,0:T(8,128)(2,1)S(1)}, u32[]{:S(2)}, u32[]{:S(2)}) collective-permute-start(bf16[128,512]{1,0:T(8,128)(2,1)S(1)} %get-tuple-element.63), channel_id=1, source_target_pairs={{0,2},{1,3},{2,0},{3,1},{4,6},{5,7},{6,4},{7,5},{8,10},{9,11},{10,... | collective-permute-start | bytes 393224 | tf_op jit(solution)/shard_map/ppermute | solution.py:32
  260.0 3.8 %copy-start.10 = (bf16[128,512]{1,0:T(8,128)(2,1)}, bf16[128,512]{1,0:T(8,128)(2,1)S(1)}, u32[]{:S(2)}) copy-start(bf16[128,512]{1,0:T(8,128)(2,1)S(1)} %collective-permute-done.16.right) | copy-start | bytes 393220
  263.7 9.6 %copy-start.8 = (bf16[128,128]{0,1:T(8,128)(2,1)S(1)}, bf16[128,128]{0,1:T(8,128)(2,1)}, u32[]{:S(2)}) copy-start(bf16[128,128]{0,1:T(8,128)(2,1)} %copy-done.7) | copy-start | bytes 98308
  263.8 13.0 %copy-start.13 = (pred[128,128]{0,1:T(32,128)(4,1)S(1)}, pred[128,128]{0,1:T(32,128)(4,1)}, u32[]{:S(2)}) copy-start(pred[128,128]{0,1:T(32,128)(4,1)} %copy-done.12) | copy-start | bytes 49156
  264.4 61.1 %all-to-all-start.3 = ((bf16[128,8,2048]{2,1,0:T(8,128)(2,1)}), bf16[128,8,2048]{2,1,0:T(8,128)(2,1)}, u32[]{:S(2)}, u32[]{:S(2)}) async-start(bf16[128,8,2048]{2,1,0:T(8,128)(2,1)} %bitcast.63), calls=%async_computation.3 | async-start | bytes 8388608 | tf_op jit(solution)/shard_map/all_to_all | solution.py:424
  (5 other events, 6.3 us)
